TPU v7x, 128 devices: a whole 4x4x4 slice. The times are simulated.
128 devices in a mesh: row: 16 (over y_hi, z, core), col: 8 (over y_lo, x).
Axes of the slice: x: 4, y: 4 (y_hi: 2, y_lo: 2; y = y_hi * 2 + y_lo), z: 4, core: 2. Of those that a mesh axis runs over, the one named last changes fastest.
Arguments:
- features: bfloat16 [65536, 128], P(('row', 'col')), may hold values from -12 to 12
- tile_values: bfloat16 [16, 8, 512, 128, 128], P('row', 'col'), as said below
- tile_rows: int32 [16, 8, 512], P('row', 'col'), may hold values from 0 to 63, as said below
- tile_cols: int32 [16, 8, 512], P('row', 'col'), may hold values from 0 to 31
- tile_count: int32 [16, 8], P('row', 'col'), may hold values from 64 to 512, as said below
- weight1: bfloat16 [128, 256], replicated, may hold values from -0.5 to 0.5
- bias1: float32 [256], replicated, may hold values from -1 to 1
- weight2: bfloat16 [256, 256], replicated
- bias2: float32 [256], replicated, may hold values from -3 to 3
Outputs:
- node_out: bfloat16 [65536, 256], P(('row', 'col'))
Inputs may be any that keep to these rules, and one draw needn't show every extreme that they name: The pairs (tile_rows, tile_cols) of one device are distinct. Slots 0 to tile_count - 1 of a device hold its nonempty tiles; later slots are padding. `tile_values`: entries are nonnegative.
All inputs are finite; a program needn't handle non-finite values.
Results may differ from a plain program's by a relative error of at most 0.0037.
Values may be sent and summed in bfloat16 or wider, within the bound.
No kernel may reach another device: no remote copies, remote signals or barrier semaphores. Data moves between devices by JAX's collectives and lax.ppermute only.
A program may use at most 192 MiB of HBM per device.

v0:
```python
import jax
import jax.numpy as jnp
from jax import lax
from jax.sharding import PartitionSpec as P


def accumulate(values, out_index, in_index, live_mask, source, out_blocks, transposed):
    tile_size = values.shape[-1]
    feature_width = source.shape[-1]
    slot_count = values.shape[0]
    group_size = min(128, slot_count)
    group_turns = slot_count // group_size
    source_blocks = source.reshape(-1, tile_size, feature_width)
    in_blocks = source_blocks.shape[0]
    unit_vector = jnp.ones((tile_size,), values.dtype)
    out_range = jnp.arange(out_blocks, dtype=jnp.int32)
    in_range = jnp.arange(in_blocks, dtype=jnp.int32)

    def advance(state, inputs):
        summed, degree = state
        tile_block, out_part, in_part, kept_mask = inputs
        select_in = (in_part[:, None] == in_range[None, :]).astype(source.dtype)
        picked = jnp.einsum(
            "gi,ibw->gbw", select_in, source_blocks, preferred_element_type=jnp.float32
        ).astype(source.dtype)
        if transposed:
            products = jnp.einsum(
                "gba,gbw->gaw", tile_block, picked, preferred_element_type=jnp.float32
            )
            tile_sums = jnp.einsum(
                "gba,b->ga", tile_block, unit_vector, preferred_element_type=jnp.float32
            )
        else:
            products = jnp.einsum(
                "gab,gbw->gaw", tile_block, picked, preferred_element_type=jnp.float32
            )
            tile_sums = jnp.einsum(
                "gab,b->ga", tile_block, unit_vector, preferred_element_type=jnp.float32
            )
        select_out = (out_part[:, None] == out_range[None, :]).astype(jnp.float32) * kept_mask[
            :, None
        ]
        summed = summed + jnp.einsum(
            "go,gaw->oaw",
            select_out,
            products,
            precision=lax.Precision.HIGHEST,
            preferred_element_type=jnp.float32,
        )
        degree = degree + jnp.einsum(
            "go,ga->oa",
            select_out,
            tile_sums,
            precision=lax.Precision.HIGHEST,
            preferred_element_type=jnp.float32,
        )
        return ((summed, degree), None)

    initial = (
        jnp.zeros((out_blocks, tile_size, feature_width), jnp.float32),
        jnp.zeros((out_blocks, tile_size), jnp.float32),
    )
    grouped = (
        values.reshape(group_turns, group_size, tile_size, tile_size),
        out_index.reshape(group_turns, group_size),
        in_index.reshape(group_turns, group_size),
        live_mask.reshape(group_turns, group_size),
    )
    (summed, degree), _ = lax.scan(advance, initial, grouped)
    return (
        summed.reshape(out_blocks * tile_size, feature_width),
        degree.reshape(out_blocks * tile_size),
    )


def self_term(source, out_start, in_start, out_length):
    positions = out_start - in_start + jnp.arange(out_length, dtype=jnp.int32)
    inside = (positions >= 0) & (positions < source.shape[0])
    picked = jnp.take(source, jnp.clip(positions, 0, source.shape[0] - 1), axis=0)
    return jnp.where(inside[:, None], picked.astype(jnp.float32), 0.0)


def local(features, tile_values, tile_rows, tile_cols, tile_count, weight1, bias1, weight2, bias2):
    row_pos = lax.axis_index("row")
    col_pos = lax.axis_index("col")
    rows_dev = features.shape[0]
    tile_size = tile_values.shape[-1]
    span_rows = rows_dev * lax.axis_size("row")
    span_cols = rows_dev * lax.axis_size("col")
    values = tile_values[0, 0]
    block_rows = tile_rows[0, 0]
    block_cols = tile_cols[0, 0]
    slot_count = values.shape[0]
    live_mask = (jnp.arange(slot_count, dtype=jnp.int32) < tile_count[0, 0]).astype(jnp.float32)
    gathered = lax.all_gather(features, "col", axis=0, tiled=True)
    first_partial, first_degree = accumulate(
        values, block_rows, block_cols, live_mask, gathered, span_rows // tile_size, False
    )
    first_partial = first_partial + self_term(
        gathered, col_pos * span_rows, row_pos * span_cols, span_rows
    )
    summed, degree_sum = (
        lax.psum_scatter(first_partial, "row", scatter_dimension=0, tiled=True),
        lax.psum_scatter(first_degree, "row", scatter_dimension=0, tiled=True),
    )
    mean_rows = (summed / (1.0 + degree_sum)[:, None]).astype(jnp.bfloat16)
    hidden_rows = lax.all_gather(
        jax.nn.relu(jnp.dot(mean_rows, weight1, preferred_element_type=jnp.float32) + bias1).astype(
            jnp.bfloat16
        ),
        "row",
        axis=0,
        tiled=True,
    )
    second_partial, second_degree = accumulate(
        values, block_cols, block_rows, live_mask, hidden_rows, span_cols // tile_size, True
    )
    second_partial = second_partial + self_term(
        hidden_rows, row_pos * span_cols, col_pos * span_rows, span_cols
    )
    second_summed, second_total = (
        lax.psum_scatter(second_partial, "col", scatter_dimension=0, tiled=True),
        lax.psum_scatter(second_degree, "col", scatter_dimension=0, tiled=True),
    )
    second_mean = (second_summed / (1.0 + second_total)[:, None]).astype(jnp.bfloat16)
    return (jnp.dot(second_mean, weight2, preferred_element_type=jnp.float32) + bias2).astype(
        jnp.bfloat16
    )


def solution(mesh):
    in_specs = (
        P(("row", "col"), None),
        P("row", "col", None, None, None),
        P("row", "col", None),
        P("row", "col", None),
        P("row", "col"),
        P(),
        P(),
        P(),
        P(),
    )
    out_specs = P(("row", "col"), None)
    return jax.shard_map(local, mesh=mesh, in_specs=in_specs, out_specs=out_specs, check_vma=False)
```

profile of v0, /device:TPU:1, one launch (start us, length us, event | category | flops | bytes accessed | tf_op | source)
XLA Modules:
  0.0 642.5 jit_solution(11154769232702023597)
XLA Ops:
  8.1 37.9 %all-gather.3.cloned.1.call-done = bf16[4096,128]{1,0:T(8,128)(2,1)} async-done(((bf16[512,128]{1,0:T(8,128)(2,1)}), bf16[4096,128]{1,0:T(8,128)(2,1)}) %all-gather.3.cloned.1.call-update) | async-done | bytes 1048592 | tf_op jit(solution)/shard_map/all_gather | solution.py:95
  46.1 1.9 copy.20
  48.0 122.9 %while.26 = (s32[]{:T(128)}, f32[64,128,128]{2,0,1:T(8,128)}, f32[64,128]{1,0:T(8,128)S(1)}, s32[4,128]{1,0:T(4,128)}, f32[4,128]{1,0:T(4,128)S(1)}, /*index=5*/...) while((s32[]{:T(128)}, f32[64,128,128]{2,0,1:T(8,128)}, ...), condition=%wide.region_1.2_spmd.clone, body=%wide.region_0.1_spmd.clone.sunk | while | flops 2302726144 | bytes 43194996 | solution.py:69
  50.0 10.0 %fusion.128 = f32[128,128,128]{2,1,0:T(8,128)} fusion(bf16[128,128,128]{2,0,1:T(8,128)(2,1)S(1)} %convolution_convert_fusion.4, bf16[4,128,128,128]{3,2,1,0:T(8,128)(2,1)} %get-tuple-element.364, s32[]{:T(128)} %get-tuple-element.349), kind=kOutput, calls=%fused_computation.10.clone.1 | convolution fusion | flops 536870912 | bytes 16777728 | tf_op jit(solution)/shard_map/while/body/eval_jaxpr/gab,gbw->gaw/dot_general | solution.py:34
  60.0 14.6 %select_add_fusion.4 = f32[64,128,128]{2,0,1:T(8,128)} fusion(f32[64,128,128]{2,0,1:T(8,128)} %get-tuple-element.350, f32[128,128,128]{2,1,0:T(8,128)} %fusion.128, pred[]{:T(512)S(6)} %compare.6, f32[128]{0:T(128)S(1)} %fusion.129, s32[128]{0:T(128)S(1)} %get-tuple-element.328), kind=kOutput, calls=%fused_computation.13.clone.1 | convolution fusion | flops 1612726272 | bytes 16778240 | tf_op jit(solution)/shard_map/while/body/eval_jaxpr/go,gaw->oaw/dot_general | solution.py:43
  74.6 3.4 fusion.130
  78.9 1.3 convolution_convert_fusion.4
  80.2 10.0 %fusion.128 = f32[128,128,128]{2,1,0:T(8,128)} fusion(bf16[128,128,128]{2,0,1:T(8,128)(2,1)S(1)} %convolution_convert_fusion.4, bf16[4,128,128,128]{3,2,1,0:T(8,128)(2,1)} %get-tuple-element.364, s32[]{:T(128)} %get-tuple-element.349), kind=kOutput, calls=%fused_computation.10.clone.1 | convolution fusion | flops 536870912 | bytes 16777728 | tf_op jit(solution)/shard_map/while/body/eval_jaxpr/gab,gbw->gaw/dot_general | solution.py:34
  90.2 15.2 %select_add_fusion.4 = f32[64,128,128]{2,0,1:T(8,128)} fusion(f32[64,128,128]{2,0,1:T(8,128)} %get-tuple-element.350, f32[128,128,128]{2,1,0:T(8,128)} %fusion.128, pred[]{:T(512)S(6)} %compare.6, f32[128]{0:T(128)S(1)} %fusion.129, s32[128]{0:T(128)S(1)} %get-tuple-element.328), kind=kOutput, calls=%fused_computation.13.clone.1 | convolution fusion | flops 1612726272 | bytes 16778240 | tf_op jit(solution)/shard_map/while/body/eval_jaxpr/go,gaw->oaw/dot_general | solution.py:43
  105.4 3.4 fusion.130
  111.0 10.0 %fusion.128 = f32[128,128,128]{2,1,0:T(8,128)} fusion(bf16[128,128,128]{2,0,1:T(8,128)(2,1)S(1)} %convolution_convert_fusion.4, bf16[4,128,128,128]{3,2,1,0:T(8,128)(2,1)} %get-tuple-element.364, s32[]{:T(128)} %get-tuple-element.349), kind=kOutput, calls=%fused_computation.10.clone.1 | convolution fusion | flops 536870912 | bytes 16777728 | tf_op jit(solution)/shard_map/while/body/eval_jaxpr/gab,gbw->gaw/dot_general | solution.py:34
  121.0 15.2 %select_add_fusion.4 = f32[64,128,128]{2,0,1:T(8,128)} fusion(f32[64,128,128]{2,0,1:T(8,128)} %get-tuple-element.350, f32[128,128,128]{2,1,0:T(8,128)} %fusion.128, pred[]{:T(512)S(6)} %compare.6, f32[128]{0:T(128)S(1)} %fusion.129, s32[128]{0:T(128)S(1)} %get-tuple-element.328), kind=kOutput, calls=%fused_computation.13.clone.1 | convolution fusion | flops 1612726272 | bytes 16778240 | tf_op jit(solution)/shard_map/while/body/eval_jaxpr/go,gaw->oaw/dot_general | solution.py:43
  136.3 3.4 fusion.130
  141.9 10.0 %fusion.128 = f32[128,128,128]{2,1,0:T(8,128)} fusion(bf16[128,128,128]{2,0,1:T(8,128)(2,1)S(1)} %convolution_convert_fusion.4, bf16[4,128,128,128]{3,2,1,0:T(8,128)(2,1)} %get-tuple-element.364, s32[]{:T(128)} %get-tuple-element.349), kind=kOutput, calls=%fused_computation.10.clone.1 | convolution fusion | flops 536870912 | bytes 16777728 | tf_op jit(solution)/shard_map/while/body/eval_jaxpr/gab,gbw->gaw/dot_general | solution.py:34
  151.9 15.2 %select_add_fusion.4 = f32[64,128,128]{2,0,1:T(8,128)} fusion(f32[64,128,128]{2,0,1:T(8,128)} %get-tuple-element.350, f32[128,128,128]{2,1,0:T(8,128)} %fusion.128, pred[]{:T(512)S(6)} %compare.6, f32[128]{0:T(128)S(1)} %fusion.129, s32[128]{0:T(128)S(1)} %get-tuple-element.328), kind=kOutput, calls=%fused_computation.13.clone.1 | convolution fusion | flops 1612726272 | bytes 16778240 | tf_op jit(solution)/shard_map/while/body/eval_jaxpr/go,gaw->oaw/dot_general | solution.py:43
  167.2 3.4 fusion.130
  170.9 6.7 %copy.21 = f32[64,128,128]{2,1,0:T(8,128)} copy(f32[64,128,128]{2,0,1:T(8,128)} %get-tuple-element.111) | data formatting | bytes 8388608 | tf_op jit(solution)/shard_map/while | solution.py:69
  177.6 24.0 %gather_fusion = bf16[8192,128]{1,0:T(8,128)(2,1)S(1)} fusion(bf16[4096,128]{1,0:T(8,128)(2,1)S(1)} %copy-done.1, s32[8192]{0:T(1024)S(1)} %broadcast_clamp_fusion), kind=kCustom, calls=%fused_computation | custom fusion | bytes 4227072 | tf_op jit(solution)/shard_map/jit(_take)/gather | solution.py:79
  201.6 8.1 %bitcast_add_fusion.1 = f32[8192,128]{1,0:T(8,128)} fusion(f32[64,128,128]{2,1,0:T(8,128)} %copy.21, bf16[8192,128]{1,0:T(8,128)(2,1)S(1)} %gather_fusion, pred[8192]{0:T(1024)(128)(4,1)S(1)} %get-tuple-element.229, pred[8192]{0:T(1024)(128)(4,1)S(1)} %get-tuple-element.230), kind=kLoop, calls=%fused_computation.79 | loop fusion | flops 4194304 | bytes 10502144 | tf_op jit(solution)/shard_map/add | solution.py:99
  211.5 65.0 %all-reduce = f32[8192]{0:T(1024)S(1)} all-reduce(f32[8192]{0:T(1024)S(1)} %bitcast.105), channel_id=3, replica_groups=mesh['row'=16,'col'=8] {'row'}, use_global_device_ids=true, to_apply=%region_3.4.clone | all-reduce | flops 8192 | bytes 65536
  276.6 16.8 %reduce-scatter.3.cloned.1.call-done = f32[512,128]{1,0:T(8,128)} async-done(((f32[8192,128]{1,0:T(8,128)}), f32[512,128]{1,0:T(8,128)}) %reduce-scatter.3.cloned.1.call-update) | async-done | bytes 262160 | tf_op jit(solution)/shard_map/reduce_scatter | solution.py:103
  293.4 1.9 fusion.69
  295.4 22.4 %copy.18 = bf16[1,1,512,128,128]{3,4,2,1,0:T(8,128)(2,1)} copy(bf16[1,1,512,128,128]{4,3,2,1,0:T(8,128)(2,1)} %bitcast.100) | data formatting | bytes 33554432 | tf_op args[1]
  317.9 34.3 %all-gather.5.cloned.1.call-done = bf16[8192,256]{1,0:T(8,128)(2,1)} async-done(((bf16[512,256]{1,0:T(8,128)(2,1)}), bf16[8192,256]{1,0:T(8,128)(2,1)}) %all-gather.5.cloned.1.call-update) | async-done | bytes 4194320 | tf_op jit(solution)/shard_map/all_gather | solution.py:107
  352.2 6.5 %copy.22 = bf16[64,128,256]{2,0,1:T(8,128)(2,1)} copy(bf16[64,128,256]{2,1,0:T(8,128)(2,1)} %bitcast.102) | data formatting | bytes 8388608
  358.7 194.5 %while.27 = (s32[]{:T(128)}, f32[32,128,256]{2,0,1:T(8,128)}, f32[32,128]{1,0:T(8,128)S(1)}, s32[4,128]{1,0:T(4,128)}, f32[4,128]{1,0:T(4,128)S(1)}, /*index=5*/...) while((s32[]{:T(128)}, f32[32,128,256]{2,0,1:T(8,128)}, ...), condition=%wide.region_5.6_spmd.clone, body=%wide.region_4.5_spmd.clone.sunk | while | flops 3238035456 | bytes 71473784 | solution.py:69
  359.6 4.6 convolution_convert_fusion.5
  364.2 13.7 %fusion.141 = f32[128,128,256]{2,1,0:T(8,128)} fusion(bf16[128,128,256]{2,0,1:T(8,128)(2,1)S(1)} %convolution_convert_fusion.5, bf16[4,128,128,128]{2,3,1,0:T(8,128)(2,1)} %get-tuple-element.394, s32[]{:T(128)} %get-tuple-element.379), kind=kOutput, calls=%fused_computation.44.clone.1 | convolution fusion | flops 1073741824 | bytes 29360640 | tf_op jit(solution)/shard_map/while/body/eval_jaxpr/gba,gbw->gaw/dot_general | solution.py:27
  377.9 25.5 %select_add_fusion.5 = f32[32,128,256]{2,0,1:T(8,128)} fusion(f32[32,128,256]{2,0,1:T(8,128)} %get-tuple-element.380, pred[]{:T(512)S(6)} %compare.7, f32[128,128,256]{2,1,0:T(8,128)} %fusion.141, f32[128]{0:T(128)S(1)} %fusion.142, s32[128]{0:T(128)S(1)} %get-tuple-element.338), kind=kOutput, calls=%fused_computation.50.clone.1 | convolution fusion | flops 1612718080 | bytes 25166848 | tf_op jit(solution)/shard_map/while/body/eval_jaxpr/go,gaw->oaw/dot_general | solution.py:43
  403.4 3.4 fusion.143
  407.7 4.6 convolution_convert_fusion.5
  412.3 13.7 %fusion.141 = f32[128,128,256]{2,1,0:T(8,128)} fusion(bf16[128,128,256]{2,0,1:T(8,128)(2,1)S(1)} %convolution_convert_fusion.5, bf16[4,128,128,128]{2,3,1,0:T(8,128)(2,1)} %get-tuple-element.394, s32[]{:T(128)} %get-tuple-element.379), kind=kOutput, calls=%fused_computation.44.clone.1 | convolution fusion | flops 1073741824 | bytes 29360640 | tf_op jit(solution)/shard_map/while/body/eval_jaxpr/gba,gbw->gaw/dot_general | solution.py:27
  426.0 26.1 %select_add_fusion.5 = f32[32,128,256]{2,0,1:T(8,128)} fusion(f32[32,128,256]{2,0,1:T(8,128)} %get-tuple-element.380, pred[]{:T(512)S(6)} %compare.7, f32[128,128,256]{2,1,0:T(8,128)} %fusion.141, f32[128]{0:T(128)S(1)} %fusion.142, s32[128]{0:T(128)S(1)} %get-tuple-element.338), kind=kOutput, calls=%fused_computation.50.clone.1 | convolution fusion | flops 1612718080 | bytes 25166848 | tf_op jit(solution)/shard_map/while/body/eval_jaxpr/go,gaw->oaw/dot_general | solution.py:43
  452.1 3.4 fusion.143
  456.4 4.6 convolution_convert_fusion.5
  460.9 13.8 %fusion.141 = f32[128,128,256]{2,1,0:T(8,128)} fusion(bf16[128,128,256]{2,0,1:T(8,128)(2,1)S(1)} %convolution_convert_fusion.5, bf16[4,128,128,128]{2,3,1,0:T(8,128)(2,1)} %get-tuple-element.394, s32[]{:T(128)} %get-tuple-element.379), kind=kOutput, calls=%fused_computation.44.clone.1 | convolution fusion | flops 1073741824 | bytes 29360640 | tf_op jit(solution)/shard_map/while/body/eval_jaxpr/gba,gbw->gaw/dot_general | solution.py:27
  474.7 26.1 %select_add_fusion.5 = f32[32,128,256]{2,0,1:T(8,128)} fusion(f32[32,128,256]{2,0,1:T(8,128)} %get-tuple-element.380, pred[]{:T(512)S(6)} %compare.7, f32[128,128,256]{2,1,0:T(8,128)} %fusion.141, f32[128]{0:T(128)S(1)} %fusion.142, s32[128]{0:T(128)S(1)} %get-tuple-element.338), kind=kOutput, calls=%fused_computation.50.clone.1 | convolution fusion | flops 1612718080 | bytes 25166848 | tf_op jit(solution)/shard_map/while/body/eval_jaxpr/go,gaw->oaw/dot_general | solution.py:43
  500.8 3.4 fusion.143
  505.0 4.6 convolution_convert_fusion.5
  509.6 13.7 %fusion.141 = f32[128,128,256]{2,1,0:T(8,128)} fusion(bf16[128,128,256]{2,0,1:T(8,128)(2,1)S(1)} %convolution_convert_fusion.5, bf16[4,128,128,128]{2,3,1,0:T(8,128)(2,1)} %get-tuple-element.394, s32[]{:T(128)} %get-tuple-element.379), kind=kOutput, calls=%fused_computation.44.clone.1 | convolution fusion | flops 1073741824 | bytes 29360640 | tf_op jit(solution)/shard_map/while/body/eval_jaxpr/gba,gbw->gaw/dot_general | solution.py:27
  523.4 26.1 %select_add_fusion.5 = f32[32,128,256]{2,0,1:T(8,128)} fusion(f32[32,128,256]{2,0,1:T(8,128)} %get-tuple-element.380, pred[]{:T(512)S(6)} %compare.7, f32[128,128,256]{2,1,0:T(8,128)} %fusion.141, f32[128]{0:T(128)S(1)} %fusion.142, s32[128]{0:T(128)S(1)} %get-tuple-element.338), kind=kOutput, calls=%fused_computation.50.clone.1 | convolution fusion | flops 1612718080 | bytes 25166848 | tf_op jit(solution)/shard_map/while/body/eval_jaxpr/go,gaw->oaw/dot_general | solution.py:43
  549.4 3.4 fusion.143
  553.2 6.6 %copy.23 = f32[32,128,256]{2,1,0:T(8,128)} copy(f32[32,128,256]{2,0,1:T(8,128)} %get-tuple-element.113) | data formatting | bytes 8388608 | tf_op jit(solution)/shard_map/while | solution.py:69
  559.8 15.7 %gather_fusion.1 = bf16[4096,256]{1,0:T(8,128)(2,1)S(1)} fusion(bf16[8192,256]{1,0:T(8,128)(2,1)} %all-gather.5.cloned.1.call-done, s32[4096]{0:T(1024)S(1)} %broadcast_clamp_fusion.1), kind=kCustom, calls=%fused_computation.1 | custom fusion | bytes 4210688 | tf_op jit(solution)/shard_map/jit(_take)/gather | solution.py:79
  575.5 6.8 %bitcast_add_fusion = f32[4096,256]{1,0:T(8,128)} fusion(f32[32,128,256]{2,1,0:T(8,128)} %copy.23, bf16[4096,256]{1,0:T(8,128)(2,1)S(1)} %gather_fusion.1, pred[4096]{0:T(1024)(128)(4,1)S(1)} %get-tuple-element.231, pred[4096]{0:T(1024)(128)(4,1)S(1)} %get-tuple-element.232), kind=kLoop, calls=%fused_computation.78 | loop fusion | flops 4194304 | bytes 10493952 | tf_op jit(solution)/shard_map/add | solution.py:118
  584.2 29.4 %all-reduce.1 = f32[4096]{0:T(1024)S(1)} all-reduce(f32[4096]{0:T(1024)S(1)} %bitcast.106), channel_id=5, replica_groups=mesh['row'=16,'col'=8] {'col'}, use_global_device_ids=true, to_apply=%region_7.8.clone | all-reduce | flops 4096 | bytes 32768
  613.7 19.8 %reduce-scatter.5.cloned.1.call-done = f32[512,256]{1,0:T(8,128)} async-done(((f32[4096,256]{1,0:T(8,128)}), f32[512,256]{1,0:T(8,128)}) %reduce-scatter.5.cloned.1.call-update) | async-done | bytes 524304 | tf_op jit(solution)/shard_map/reduce_scatter | solution.py:122
  633.5 2.0 fusion.70
  (64 shorter events, 14.7 us)
Async XLA Ops:
  6.5 627.0 %copy-start = (bf16[256,256]{1,0:T(8,128)(2,1)S(1)}, bf16[256,256]{1,0:T(8,128)(2,1)}, u32[]{:S(2)}) copy-start(bf16[256,256]{1,0:T(8,128)(2,1)} %param.20) | copy-start | bytes 393220
  6.5 39.5 %all-gather.3.cloned.1.call-start = ((), (), s32[]{:S(2)}) async-start(), calls=%async_computation.2 | async-start | bytes 1179648 | tf_op jit(solution)/shard_map/all_gather | solution.py:95
  7.3 286.1 %reduce-scatter.3.cloned.1.call-start = ((), (), s32[]{:S(2)}) async-start(), calls=%async_computation.3 | async-start | bytes 4456448 | tf_op jit(solution)/shard_map/reduce_scatter | solution.py:103
  170.9 6.7 %copy-start.1 = (bf16[4096,128]{1,0:T(8,128)(2,1)S(1)}, bf16[4096,128]{1,0:T(8,128)(2,1)}, u32[]{:S(2)}) copy-start(bf16[4096,128]{1,0:T(8,128)(2,1)} %all-gather.3.cloned.1.call-done) | copy-start | bytes 3145732
  209.7 0.7 copy-start.6
  209.7 83.8 %copy-start.2 = (bf16[128,256]{1,0:T(8,128)(2,1)S(1)}, bf16[128,256]{1,0:T(8,128)(2,1)}, u32[]{:S(2)}) copy-start(bf16[128,256]{1,0:T(8,128)(2,1)} %param.18) | copy-start | bytes 196612
  209.7 83.8 %copy-start.3 = (f32[256]{0:T(256)S(1)}, f32[256]{0:T(256)}, u32[]{:S(2)}) copy-start(f32[256]{0:T(256)} %param.19) | copy-start | bytes 3076
  209.7 142.5 %all-gather.5.cloned.1.call-start = ((), (), s32[]{:S(2)}) async-start(), calls=%async_computation.4 | async-start | bytes 4456448 | tf_op jit(solution)/shard_map/all_gather | solution.py:107
  295.4 338.1 %reduce-scatter.5.cloned.1.call-start = ((), (), s32[]{:S(2)}) async-start(), calls=%async_computation.5 | async-start | bytes 4718592 | tf_op jit(solution)/shard_map/reduce_scatter | solution.py:122
  582.4 0.7 copy-start.5
  582.4 51.2 %copy-start.4 = (f32[256]{0:T(256)S(1)}, f32[256]{0:T(256)}, u32[]{:S(2)}) copy-start(f32[256]{0:T(256)} %param.21) | copy-start | bytes 3076
Sparse Core Ops, SparseCore 0:
  9.0 37.0 all-gather.2
  209.8 83.5 reduce-scatter.2
  296.2 55.9 all-gather.4
  582.5 50.9 reduce-scatter.4
where the time goes:
time: 653 us; the launch traced here: 643 us
  matrix products  315 us (48%)
  waiting for transfers between devices  110 us (17%)
  blocking collectives  94.4 us (14%)
  local copies, waits for them, and re-layouts  91.8 us (14%)
  between operations  15.7 us (2%)
  other arithmetic  15.2 us (2%)
    dot_general x8, matrix products, advance(): jnp.einsum('go,gaw->oaw', select_out, products, precision=lax.Precision.H...  164 us
    unnamed x2, blocking collectives  94.4 us
    dot_general x4, matrix products, advance(): jnp.einsum('gba,gbw->gaw', tile_block, picked, preferred_element_type=jnp...  55 us
    dot_general x4, matrix products, advance(): jnp.einsum('gab,gbw->gaw', tile_block, picked, preferred_element_type=jnp...  40 us
    gather x2, local copies, waits for them, and re-layouts, self_term(): jnp.take(source, jnp.clip(positions, 0, source.shape[0] - 1), axis=0)  39.7 us
    all_gather x1, waiting for transfers between devices, local(): gathered = lax.all_gather(features, 'col', axis=0, tiled=True)  37.9 us
    all_gather x1, waiting for transfers between devices, local(): lax.all_gather(jax.nn.relu(jnp.dot(mean_rows, weight1, preferred_element_...  34.3 us
    unnamed x19, local copies, waits for them, and re-layouts  33.2 us
  transfers between devices with their start and end apart: 4, of which 4 were waited for; matrix products, arithmetic and copies ran while one was open for 4% of the time, Pallas kernels for 0%

commit v1 on v0

v1 whole, which is shorter than its diff:
```python
import functools

import jax
import jax.numpy as jnp
from jax import lax
from jax.experimental import pallas as pl
from jax.experimental.pallas import tpu as pltpu
from jax.sharding import PartitionSpec as P

F32 = jnp.float32
BF16 = jnp.bfloat16
I32 = jnp.int32
TILE = 128
EXTRA = 16
UNROLL = 8
CHUNK = 32


def dot(a, b, dims):
    return lax.dot_general(a, b, (dims, ((), ())), preferred_element_type=F32)


def order_by(key_row, key_col, other_col, slot_col, live_col, blocks, length, other_span):
    slots = key_col.shape[0]
    lane_block = lax.broadcasted_iota(I32, (slots, 128), 1)
    hot = jnp.where((key_col == lane_block) & (live_col > 0), 1.0, 0.0)
    before = jnp.where(
        lax.broadcasted_iota(I32, (slots, slots), 1) < lax.broadcasted_iota(I32, (slots, slots), 0), 1.0, 0.0
    )
    prefix = dot(before.astype(BF16), hot.astype(BF16), ((1,), (0,)))
    rank = jnp.sum(hot * prefix, axis=1, keepdims=True)
    count = jnp.sum(hot, axis=0, keepdims=True)
    pairs = jnp.floor((count + 1.0) * 0.5)
    below = jnp.where(
        lax.broadcasted_iota(I32, (128, 128), 0) < lax.broadcasted_iota(I32, (128, 128), 1), 1.0, 0.0
    )
    start = dot(jnp.broadcast_to(pairs, (8, 128)).astype(BF16), below.astype(BF16), ((1,), (0,)))[0:1]
    place = 2.0 * jnp.sum(hot * start, axis=1, keepdims=True) + rank
    place = jnp.where(live_col > 0, place, -1.0).astype(I32)
    empty = slots * other_span
    code = slot_col * other_span + other_col - empty
    where_to = lax.broadcasted_iota(I32, (slots, length), 1)
    codes = jnp.sum(jnp.where(place == where_to, code, 0), axis=0, keepdims=True) + empty
    start_col = jnp.transpose(jnp.broadcast_to(start, (8, 128)))[:, 0:1]
    block_id = lax.broadcasted_iota(I32, (128, length), 0)
    pair_id = lax.broadcasted_iota(I32, (128, length), 1).astype(F32)
    reached = (start_col <= pair_id) & (block_id < blocks)
    out_block = jnp.sum(jnp.where(reached, 1, 0), axis=0, keepdims=True) - 1
    total = jnp.sum(pairs, axis=1, keepdims=True).astype(I32)
    return codes, out_block, total


def order_kernel(row_blocks, col_blocks, count_ref, index_ref, list_ref):
    slots = index_ref.shape[1]
    length = list_ref.shape[1]
    turned = jnp.transpose(index_ref[...].astype(F32)).astype(I32)
    row_col, col_col = turned[:, 0:1], turned[:, 1:2]
    slot_col = lax.broadcasted_iota(I32, (slots, 1), 0)
    live_col = jnp.where(slot_col < count_ref[0, 0], 1, 0)
    lists = []
    for key, other, blocks, span in (
        (row_col, col_col, row_blocks, 64),
        (col_col, row_col, col_blocks, 64),
    ):
        codes, out_block, total = order_by(None, key, other, slot_col, live_col, blocks, length, span)
        lists += [codes, out_block, jnp.broadcast_to(total, (1, length))]
    list_ref[...] = jnp.concatenate(lists + [lists[0], lists[0]], axis=0)


def load_tiles(values_ref, tiles, sems, count):
    slots = values_ref.shape[0]
    steps = slots // CHUNK
    copies = [
        pltpu.make_async_copy(
            values_ref.at[pl.ds(i * CHUNK, CHUNK)], tiles.at[pl.ds(i * CHUNK, CHUNK)], sems.at[i]
        )
        for i in range(steps)
    ]
    for i, copy in enumerate(copies):
        pl.when(i * CHUNK < count)(copy.start)
    tiles[slots] = jnp.zeros(tiles.shape[1:], tiles.dtype)

    def finish():
        for i, copy in enumerate(copies):
            pl.when(i * CHUNK < count)(copy.wait)

    return finish


def run_pairs(list_ref, first, tiles, source, acc, tile_dims):
    total = list_ref[first + 2, 0]
    ones = jnp.ones((EXTRA, 2 * TILE), BF16)

    def step(i, carry):
        sums = []
        for u in range(UNROLL):
            q = i * UNROLL + u
            code0 = list_ref[first, 2 * q]
            code1 = list_ref[first, 2 * q + 1]
            left = jnp.concatenate([source[code0 & 63], source[code1 & 63]], axis=1)
            left = jnp.concatenate([left, ones], axis=0)
            axis = 0 if tile_dims == 0 else 1
            right = jnp.concatenate([tiles[code0 >> 6], tiles[code1 >> 6]], axis=axis)
            sums.append(dot(left, right, ((1,), (tile_dims,))))
        for u in range(UNROLL):
            block = list_ref[first + 1, i * UNROLL + u]
            acc[block] += sums[u]
        return carry

    lax.fori_loop(0, (total + UNROLL - 1) // UNROLL, step, 0)


def write_partials(acc, out_ref, per_dest, width):
    def one(d, carry):
        tails = []
        for j in range(per_dest):
            block = acc[d * per_dest + j]
            out_ref[d, pl.ds(j * width, width), :] = block[:width].astype(BF16)
            degree = block[width : width + 1]
            high = degree.astype(BF16).astype(F32)
            tails += [high, degree - high]
        tails.append(jnp.zeros((EXTRA - 2 * per_dest, TILE), F32))
        out_ref[d, pl.ds(per_dest * width, EXTRA), :] = jnp.concatenate(tails, axis=0).astype(BF16)
        return carry

    lax.fori_loop(0, out_ref.shape[0], one, 0)


def own_region(per_row):
    row, col = lax.axis_index("row"), lax.axis_index("col")
    return row // per_row == col, row % per_row


def first_kernel(per_row, count_ref, list_ref, source_ref, values_ref, out_ref, tiles, acc, sems):
    finish = load_tiles(values_ref, tiles, sems, count_ref[0, 0])
    acc[...] = jnp.zeros_like(acc)
    own, part = own_region(per_row)
    col_blocks = source_ref.shape[0]

    @pl.when(own)
    def _():
        def add(j, carry):
            acc[part * col_blocks + j, pl.ds(0, TILE), :] = source_ref[j].astype(F32)
            return carry

        lax.fori_loop(0, col_blocks, add, 0)

    finish()
    run_pairs(list_ref, 0, tiles, source_ref, acc, 1)
    write_partials(acc, out_ref, acc.shape[0] // out_ref.shape[0], TILE)


def second_kernel(
    per_row, count_ref, list_ref, mean_ref, weight_ref, bias_ref, values_ref, out_ref, tiles, acc, hidden, sems
):
    finish = load_tiles(values_ref, tiles, sems, count_ref[0, 0])
    width = hidden.shape[1]
    bias = jnp.broadcast_to(bias_ref[...], (width, TILE))

    def transform(j, carry):
        for u in range(4):
            part = dot(weight_ref[...], mean_ref[j * 4 + u], ((1,), (0,)))
            hidden[j * 4 + u] = jnp.maximum(part + bias, 0.0).astype(BF16)
        return carry

    lax.fori_loop(0, hidden.shape[0] // 4, transform, 0)
    acc[...] = jnp.zeros_like(acc)
    own, part = own_region(per_row)
    col_blocks = acc.shape[0]

    @pl.when(own)
    def _():
        def add(j, carry):
            acc[j, pl.ds(0, width), :] = hidden[part * col_blocks + j].astype(F32)
            return carry

        lax.fori_loop(0, col_blocks, add, 0)

    finish()
    run_pairs(list_ref, 3, tiles, hidden, acc, 0)
    write_partials(acc, out_ref, acc.shape[0] // out_ref.shape[0], width)


def total_mean(parts_ref, j, per_dest, width):
    sources = parts_ref.shape[0]
    block = parts_ref[0, pl.ds(j * width, width), :].astype(F32)
    for s in range(1, sources):
        block += parts_ref[s, pl.ds(j * width, width), :].astype(F32)
    tail = parts_ref[0, pl.ds(per_dest * width, EXTRA), :].astype(F32)
    for s in range(1, sources):
        tail += parts_ref[s, pl.ds(per_dest * width, EXTRA), :].astype(F32)
    degree = 1.0 + (tail[2 * j : 2 * j + 1] + tail[2 * j + 1 : 2 * j + 2])
    return (block / degree).astype(BF16)


def mean_kernel(per_dest, parts_ref, out_ref):
    for j in range(per_dest):
        mean = total_mean(parts_ref, j, per_dest, TILE)
        for d in range(out_ref.shape[0]):
            out_ref[d, j] = mean


def last_kernel(per_dest, width, parts_ref, weight_ref, bias_ref, out_ref):
    for j in range(per_dest):
        mean = total_mean(parts_ref, j, per_dest, width)
        result = dot(mean, weight_ref[...], ((0,), (0,))) + bias_ref[...]
        out_ref[pl.ds(j * TILE, TILE), :] = result.astype(BF16)


def call(kernel, out, specs, scratch=(), limit=16):
    return pl.pallas_call(
        kernel,
        out_shape=out,
        in_specs=specs,
        out_specs=pl.BlockSpec(memory_space=pltpu.VMEM),
        scratch_shapes=scratch,
        compiler_params=pltpu.CompilerParams(vmem_limit_bytes=limit * 1024 * 1024),
    )


def local(features, tile_values, tile_rows, tile_cols, tile_count, weight1, bias1, weight2, bias2):
    n_row, n_col = lax.axis_size("row"), lax.axis_size("col")
    rows_dev, in_width = features.shape
    width = weight1.shape[1]
    values = tile_values[0, 0]
    slots = values.shape[0]
    per_dev = rows_dev // TILE
    row_blocks, col_blocks = per_dev * n_row, per_dev * n_col
    per_row = n_row // n_col
    count = tile_count.astype(I32)
    vmem = pl.BlockSpec(memory_space=pltpu.VMEM)
    smem = pl.BlockSpec(memory_space=pltpu.SMEM)
    anywhere = pl.BlockSpec(memory_space=pl.ANY)

    index = jnp.concatenate([tile_rows[0], tile_cols[0], jnp.zeros((6, slots), I32)], axis=0)
    length = -(-(slots + row_blocks + 2 * UNROLL) // 128) * 128
    lists = call(
        functools.partial(order_kernel, row_blocks, col_blocks),
        jax.ShapeDtypeStruct((8, length), I32),
        [smem, vmem],
    )(count, index)

    turned = jnp.swapaxes(features.reshape(per_dev, TILE, in_width), 1, 2)
    gathered = lax.all_to_all(jnp.broadcast_to(turned[None], (n_col,) + turned.shape), "col", 0, 0)
    source = gathered.reshape(col_blocks, in_width, TILE)

    tiles = pltpu.VMEM((slots + 1, TILE, TILE), BF16)
    sems = pltpu.SemaphoreType.DMA((slots // CHUNK,))
    first = call(
        functools.partial(first_kernel, per_row),
        jax.ShapeDtypeStruct((n_row, per_dev * in_width + EXTRA, TILE), BF16),
        [smem, smem, vmem, anywhere],
        [tiles, pltpu.VMEM((row_blocks, in_width + EXTRA, TILE), F32), sems],
        48,
    )(count, lists, source, values)
    first = lax.all_to_all(first, "row", 0, 0)
    mean = call(
        functools.partial(mean_kernel, per_dev),
        jax.ShapeDtypeStruct((n_row, per_dev, in_width, TILE), BF16),
        [vmem],
    )(first)
    means = lax.all_to_all(mean, "row", 0, 0).reshape(row_blocks, in_width, TILE)
    second = call(
        functools.partial(second_kernel, per_row),
        jax.ShapeDtypeStruct((n_col, per_dev * width + EXTRA, TILE), BF16),
        [smem, smem, vmem, vmem, vmem, anywhere],
        [
            tiles,
            pltpu.VMEM((col_blocks, width + EXTRA, TILE), F32),
            pltpu.VMEM((row_blocks, width, TILE), BF16),
            sems,
        ],
        48,
    )(count, lists, means, weight1.T, bias1.reshape(width, 1), values)
    second = lax.all_to_all(second, "col", 0, 0)
    return call(
        functools.partial(last_kernel, per_dev, width),
        jax.ShapeDtypeStruct((rows_dev, width), BF16),
        [vmem, vmem, vmem],
    )(second, weight2, bias2.reshape(1, width))


def solution(mesh):
    in_specs = (
        P(("row", "col"), None),
        P("row", "col", None, None, None),
        P("row", "col", None),
        P("row", "col", None),
        P("row", "col"),
        P(),
        P(),
        P(),
        P(),
    )
    out_specs = P(("row", "col"), None)
    return jax.shard_map(local, mesh=mesh, in_specs=in_specs, out_specs=out_specs, check_vma=False)
```

time: 653 us -> 157 us (0.24)
  the two profiles are of different devices: /device:TPU:1 before, /device:TPU:0 now
where the time goes in v1:
time: 157 us; the launch traced here: 156 us
  blocking collectives  80.8 us (51%)
  waiting for transfers between devices  42.3 us (27%)
  Pallas kernels  19.2 us (12%)
  starting transfers between devices  9.24 us (6%)
  local copies, waits for them, and re-layouts  3.94 us (3%)
    all_to_all x1, blocking collectives, local(): second = lax.all_to_all(second, 'col', 0, 0)  40.9 us
    all_to_all x1, blocking collectives, local(): first = lax.all_to_all(first, 'row', 0, 0)  39.8 us
    all_to_all x1, waiting for transfers between devices, local(): lax.all_to_all(mean, 'row', 0, 0).reshape(row_blocks, in_width, TILE)  29 us
    all_to_all x1, waiting for transfers between devices, local(): lax.all_to_all(jnp.broadcast_to(turned[None], (n_col,) + turned.shape), '...  13.3 us
    pallas_call x1, Pallas kernels, local(): call(functools.partial(second_kernel, per_row), jax.ShapeDtypeStruct((n_c...  9.47 us
    pallas_call x1, Pallas kernels, local(): call(functools.partial(first_kernel, per_row), jax.ShapeDtypeStruct((n_ro...  6.52 us
    all_to_all x1, starting transfers between devices, local(): lax.all_to_all(jnp.broadcast_to(turned[None], (n_col,) + turned.shape), '...  5.4 us
    all_to_all x1, starting transfers between devices, local(): lax.all_to_all(mean, 'row', 0, 0).reshape(row_blocks, in_width, TILE)  3.85 us
  transfers between devices with their start and end apart: 2, of which 2 were waited for; matrix products, arithmetic and copies ran while one was open for 0% of the time, Pallas kernels for 1%

profile of v1, /device:TPU:0, one launch (start us, length us, event | category | flops | bytes accessed | tf_op | source)
XLA Modules:
  0.0 156.2 jit_solution(8445281379598586078)
XLA Ops:
  0.0 0.0 copy-start.5
  0.0 0.0 copy-start.4
  0.0 1.0 copy.12
  1.1 1.2 broadcast_in_dim.10
  2.3 5.4 %all-to-all-start = ((bf16[8,4,128,128]{3,2,1,0:T(8,128)(2,1)}), bf16[8,4,128,128]{3,2,1,0:T(8,128)(2,1)S(1)}, u32[]{:S(2)}, u32[]{:S(2)}) async-start(bf16[8,4,128,128]{3,2,1,0:T(8,128)(2,1)} %broadcast_in_dim.10), calls=%async_computation | async-start | bytes 2097152 | tf_op jit(solution)/shard_map/all_to_all | solution.py:244
  8.3 0.1 pad.2.clone
  8.4 0.0 copy-done.5
  8.4 0.0 copy-done.4
  8.4 0.1 add_add_fusion.index_ref
  8.5 1.6 %shard_map.91.list_ref = s32[8,640]{1,0:T(8,128)S(1)} custom-call(s32[1,1]{1,0:T(1,128)S(6)} %copy.15.count_ref, s32[8,512]{1,0:T(8,128)S(1)} %add_add_fusion.index_ref), custom_call_target="tpu_custom_call" | custom-call | tf_op jit(solution)/shard_map/pallas_call | solution.py:237
  10.1 13.3 %all-to-all-done = bf16[8,4,128,128]{3,2,1,0:T(8,128)(2,1)S(1)} async-done(((bf16[8,4,128,128]{3,2,1,0:T(8,128)(2,1)}), bf16[8,4,128,128]{3,2,1,0:T(8,128)(2,1)S(1)}, u32[]{:S(2)}, u32[]{:S(2)}) %all-to-all-start) | async-done | bytes 1048608 | tf_op jit(solution)/shard_map/all_to_all | solution.py:244
  23.4 6.5 %shard_map.92 = bf16[16,528,128]{2,1,0:T(8,128)(2,1)S(1)} custom-call(s32[1,1]{1,0:T(1,128)S(6)} %copy.15.count_ref, s32[8,640]{1,0:T(8,128)S(1)} %shard_map.91.list_ref, bf16[32,128,128]{2,1,0:T(8,128)(2,1)S(1)} %bitcast.12, bf16[512,128,128]{2,1,0:T(8,128)(2,1)} %bitcast.15), custom_call_target="tpu_custom_call" | custom-call | tf_op jit(solution)/shard_map/pallas_call | solution.py:249
  29.9 39.8 %all_to_all.20.parts_ref = bf16[16,528,128]{2,1,0:T(8,128)(2,1)S(1)} all-to-all(bf16[16,528,128]{2,1,0:T(8,128)(2,1)S(1)} %shard_map.92), channel_id=1, replica_groups=mesh['row'=16,'col'=8] {'row'}, dimensions={0} | all-to-all | bytes 4325376 | tf_op jit(solution)/shard_map/all_to_all | solution.py:256
  69.7 0.4 shard_map.93
  70.1 0.0 copy-start
  70.1 1.3 copy-done
  71.4 0.0 copy-start.6
  71.4 0.0 copy-start.3
  71.5 3.8 %all-to-all-start.2 = ((bf16[16,4,128,128]{3,2,1,0:T(8,128)(2,1)}), bf16[16,4,128,128]{3,2,1,0:T(8,128)(2,1)S(1)}, u32[]{:S(2)}, u32[]{:S(2)}) async-start(bf16[16,4,128,128]{3,2,1,0:T(8,128)(2,1)} %copy-done), calls=%async_computation.2 | async-start | bytes 4194304 | tf_op jit(solution)/shard_map/all_to_all | solution.py:262
  75.3 0.0 copy-done.6
  75.3 0.1 copy.14.bias_ref
  75.5 0.0 copy-done.3
  75.5 0.1 copy.13
  75.6 29.0 %all-to-all-done.2 = bf16[16,4,128,128]{3,2,1,0:T(8,128)(2,1)S(1)} async-done(((bf16[16,4,128,128]{3,2,1,0:T(8,128)(2,1)}), bf16[16,4,128,128]{3,2,1,0:T(8,128)(2,1)S(1)}, u32[]{:S(2)}, u32[]{:S(2)}) %all-to-all-start.2) | async-done | bytes 2097184 | tf_op jit(solution)/shard_map/all_to_all | solution.py:262
  104.6 9.5 %shard_map.94 = bf16[8,1040,128]{2,1,0:T(8,128)(2,1)S(1)} custom-call(s32[1,1]{1,0:T(1,128)S(6)} %copy.15.count_ref, s32[8,640]{1,0:T(8,128)S(1)} %shard_map.91.list_ref, bf16[64,128,128]{2,1,0:T(8,128)(2,1)S(1)} %bitcast.11, bf16[256,128]{1,0:T(8,128)(2,1)S(1)} %bitcast.13, f32[256,1]{1,0:T(8,128)S(1)} %copy.14.bias_ref, bf16[512,128,128]{2,1,0:T(8,128)(2,1)} %bitcast.16), custom_call_target="tpu_custom_call" | custom-call | tf_op jit(solution)/shard_map/pallas_call | solution.py:263
  114.1 0.0 copy-start.1
  114.1 0.0 copy-start.2
  114.1 40.9 %all_to_all.21.parts_ref = bf16[8,1040,128]{2,1,0:T(8,128)(2,1)S(1)} all-to-all(bf16[8,1040,128]{2,1,0:T(8,128)(2,1)S(1)} %shard_map.94), channel_id=1, replica_groups=mesh['row'=16,'col'=8] {'col'}, dimensions={0} | all-to-all | bytes 4259840 | tf_op jit(solution)/shard_map/all_to_all | solution.py:275
  155.0 0.0 copy-done.1
  155.0 0.0 copy-done.2
  155.0 1.2 shard_map.95
  (1 shorter events, 0.0 us)
Async XLA Ops:
  0.0 8.4 %copy-start.5 = (s32[1,1,512]{2,1,0:T(1,128)S(1)}, s32[1,1,512]{2,1,0:T(1,128)}, u32[]{:S(2)}) copy-start(s32[1,1,512]{2,1,0:T(1,128)} %param.11) | copy-start | bytes 6148
  0.0 8.4 %copy-start.4 = (s32[1,1,512]{2,1,0:T(1,128)S(1)}, s32[1,1,512]{2,1,0:T(1,128)}, u32[]{:S(2)}) copy-start(s32[1,1,512]{2,1,0:T(1,128)} %param.12) | copy-start | bytes 6148
  2.3 21.1 %all-to-all-start = ((bf16[8,4,128,128]{3,2,1,0:T(8,128)(2,1)}), bf16[8,4,128,128]{3,2,1,0:T(8,128)(2,1)S(1)}, u32[]{:S(2)}, u32[]{:S(2)}) async-start(bf16[8,4,128,128]{3,2,1,0:T(8,128)(2,1)} %broadcast_in_dim.10), calls=%async_computation | async-start | bytes 2097152 | tf_op jit(solution)/shard_map/all_to_all | solution.py:244
  70.1 1.3 copy-start
  71.4 3.9 %copy-start.6 = (f32[256]{0:T(256)S(1)}, f32[256]{0:T(256)}, u32[]{:S(2)}) copy-start(f32[256]{0:T(256)} %param.15) | copy-start | bytes 3076
  71.4 4.0 %copy-start.3 = (bf16[128,256]{1,0:T(8,128)(2,1)S(1)}, bf16[128,256]{1,0:T(8,128)(2,1)}, u32[]{:S(2)}) copy-start(bf16[128,256]{1,0:T(8,128)(2,1)} %param.14) | copy-start | bytes 196612
  71.5 33.1 %all-to-all-start.2 = ((bf16[16,4,128,128]{3,2,1,0:T(8,128)(2,1)}), bf16[16,4,128,128]{3,2,1,0:T(8,128)(2,1)S(1)}, u32[]{:S(2)}, u32[]{:S(2)}) async-start(bf16[16,4,128,128]{3,2,1,0:T(8,128)(2,1)} %copy-done), calls=%async_computation.2 | async-start | bytes 4194304 | tf_op jit(solution)/shard_map/all_to_all | solution.py:262
  114.1 41.0 %copy-start.1 = (bf16[256,256]{1,0:T(8,128)(2,1)S(1)}, bf16[256,256]{1,0:T(8,128)(2,1)}, u32[]{:S(2)}) copy-start(bf16[256,256]{1,0:T(8,128)(2,1)} %weight_ref.1) | copy-start | bytes 393220
  114.1 41.0 %copy-start.2 = (f32[256]{0:T(256)S(1)}, f32[256]{0:T(256)}, u32[]{:S(2)}) copy-start(f32[256]{0:T(256)} %param.17) | copy-start | bytes 3076
